TPU v7x, 32 devices: a whole 2x2x4 slice. The times are simulated.
32 devices in a mesh: pair: 8 (over z, x), sect: 4 (over y, core).
Axes of the slice: x: 2, y: 2, z: 4, core: 2. Of those that a mesh axis runs over, the one named last changes fastest.
Arguments:
- operators: float32 [16, 1024, 1024], P('pair', 'sect'), may hold values from -6 to 6
- rotations: float32 [8, 1024, 768], P('pair', 'sect'), may hold values from -0.1875 to 0.1875
- sector_owner: int32 [1], replicated, may hold values from 0 to 7
- slot_pair: int32 [16], replicated, may hold values from 0 to 15, each once
- sources: int32 [16, 16], replicated, may hold values from 0 to 15
- integrals: float32 [16, 16], replicated, may hold values from -3 to 3
- term_count: int32 [16], replicated, may hold values from 1 to 16, 64 in all
Outputs:
- complement: float32 [16, 768, 768], P('pair', 'sect')
Inputs may be any that keep to these rules, and one draw needn't show every extreme that they name: `sector_owner`: a pair index along the pair axis. `slot_pair`: each orbital-pair id appears once. `sources`: ids may repeat within a list. `term_count`: the counts sum to 64 and the largest is exactly 16.
All inputs are finite; a program needn't handle non-finite values.
Results may differ from a plain program's by a relative error of at most 0.0001.
Values sent between devices are 32-bit elements; how exact they have to be, the bound alone decides.
A program may use at most 64 MiB of HBM per device.

v0:
```python
import jax
import jax.numpy as jnp
from jax import lax
from jax.sharding import PartitionSpec as P


def broadcast(value, axis, root):
    mine = lax.axis_index(axis) == root
    return lax.psum(jnp.where(mine, value, jnp.zeros_like(value)), axis)


def coupling_matrix(slot_pair, sources, integrals, term_count):
    is_live = lax.broadcasted_iota(jnp.int32, sources.shape, 1) < term_count[:, None]
    weighted = jnp.where(is_live, integrals, jnp.zeros_like(integrals))
    matches = (sources[:, :, None] == slot_pair[None, None, :]).astype(jnp.float32)
    return jnp.sum(weighted[:, :, None] * matches, axis=1)


def on_device(operators, rotations, sector_owner, slot_pair, sources, integrals, term_count):
    owner_rank = sector_owner[0]
    own_block = broadcast(rotations[0], "pair", owner_rank)
    rotation_full = lax.all_gather(own_block, "sect", axis=0, tiled=True)
    sect_count = lax.axis_size("sect")
    pair_count = lax.axis_size("pair")
    local_ops = operators.shape[0]
    width_new = rotation_full.shape[1]
    new_rows = width_new // sect_count
    right_done = jnp.einsum(
        "oij,jb->oib",
        operators,
        rotation_full,
        precision=lax.Precision.HIGHEST,
        preferred_element_type=jnp.float32,
    )
    columns = lax.dynamic_slice_in_dim(
        rotation_full, lax.axis_index("sect") * new_rows, new_rows, 1
    )
    rotated = jnp.einsum(
        "ia,oib->oab",
        columns,
        lax.all_gather(right_done, "sect", axis=1, tiled=True),
        precision=lax.Precision.HIGHEST,
        preferred_element_type=jnp.float32,
    )
    coupling = coupling_matrix(slot_pair, sources, integrals, term_count)
    blocks = rotated.reshape(local_ops, pair_count, -1)
    mixture = jnp.einsum(
        "or,rhn->ohn",
        coupling,
        lax.all_to_all(blocks, "pair", split_axis=1, concat_axis=0, tiled=True),
        precision=lax.Precision.HIGHEST,
        preferred_element_type=jnp.float32,
    )
    result = lax.all_to_all(mixture, "pair", split_axis=0, concat_axis=1, tiled=True)
    return result.reshape(local_ops, new_rows, width_new)


def solution(mesh):
    in_specs = (P("pair", "sect", None), P("pair", "sect", None), P(), P(), P(), P(), P())
    out_specs = P("pair", "sect", None)
    return jax.shard_map(
        on_device, mesh=mesh, in_specs=in_specs, out_specs=out_specs, check_vma=False
    )
```

profile of v0, /device:TPU:16, one launch (start us, length us, event | category | flops | bytes accessed | tf_op | source)
XLA Modules:
  0.0 264.0 jit_solution(2301230459621125505)
XLA Ops:
  7.3 1.4 copy.18
  8.7 0.9 select_bitcast_fusion
  9.7 0.0 all-reduce.2.cloned.1.call-update
  9.7 0.0 all-gather.3.cloned.1.call-start
  9.8 75.5 %all-reduce.2.cloned.1.call-done = f32[256,768]{0,1:T(8,128)} async-done(((f32[256,768]{0,1:T(8,128)}), f32[256,768]{0,1:T(8,128)}) %all-reduce.2.cloned.1.call-update) | async-done | bytes 786448 | tf_op jit(solution)/shard_map/psum | solution.py:9
  85.2 0.0 all-gather.3.cloned.1.call-update
  85.3 0.0 all-gather.5.cloned.1.call-start
  85.3 30.6 %all-gather.3.cloned.1.call-done = f32[1024,768]{0,1:T(8,128)} async-done(((f32[256,768]{0,1:T(8,128)}), f32[1024,768]{0,1:T(8,128)}) %all-gather.3.cloned.1.call-update) | async-done | bytes 3145744 | tf_op jit(solution)/shard_map/all_gather | solution.py:22
  115.9 8.1 %fusion.2 = f32[2,256,768]{1,2,0:T(8,128)} fusion(f32[2,256,1024]{2,1,0:T(8,128)S(1)} %copy-done, f32[1024,768]{0,1:T(8,128)} %all-gather.3.cloned.1.call-done), kind=kOutput, calls=%fused_computation.3 | convolution fusion | flops 4831838208 | bytes 6815744 | tf_op jit(solution)/shard_map/oij,jb->oib/dot_general | solution.py:28
  124.0 0.0 all-gather.5.cloned.1.call-update
  124.1 46.5 %all-gather.5.cloned.1.call-done = f32[2,1024,768]{1,2,0:T(8,128)} async-done(((f32[2,256,768]{1,2,0:T(8,128)}), f32[2,1024,768]{1,2,0:T(8,128)}) %all-gather.5.cloned.1.call-update) | async-done | bytes 6291472 | tf_op jit(solution)/shard_map/all_gather | solution.py:41
  170.6 10.6 %convolution_bitcast_fusion.1 = f32[2,192,768]{2,1,0:T(8,128)} fusion(f32[2,1024,768]{1,2,0:T(8,128)} %all-gather.5.cloned.1.call-done, f32[1024,768]{0,1:T(8,128)} %all-gather.3.cloned.1.call-done, s32[]{:T(128)S(6)} %select_n.22), kind=kOutput, calls=%fused_computation.4 | convolution fusion | flops 3623878656 | bytes 8257540 | tf_op jit(solution)/shard_map/ia,oib->oab/dot_general | solution.py:38
  181.1 1.4 reshape.19
  182.6 1.9 copy.20
  184.5 6.2 %all-to-all-start = ((f32[2,8,18432]{2,0,1:T(2,128)}), f32[2,8,18432]{2,0,1:T(2,128)S(1)}, u32[]{:S(2)}, u32[]{:S(2)}) async-start(f32[2,8,18432]{2,0,1:T(2,128)} %copy.20), calls=%async_computation | async-start | bytes 2359296 | tf_op jit(solution)/shard_map/all_to_all | solution.py:50
  190.7 0.1 fusion.7
  190.8 0.1 select_reduce_fusion
  190.9 25.5 %all-to-all-done = f32[2,8,18432]{2,0,1:T(2,128)S(1)} async-done(((f32[2,8,18432]{2,0,1:T(2,128)}), f32[2,8,18432]{2,0,1:T(2,128)S(1)}, u32[]{:S(2)}, u32[]{:S(2)}) %all-to-all-start) | async-done | bytes 1179680 | tf_op jit(solution)/shard_map/all_to_all | solution.py:50
  216.4 1.8 reshape.20
  218.3 2.4 convolution_bitcast_fusion
  220.6 1.2 copy.21
  221.8 33.8 %all_to_all.30 = f32[16,1,18432]{2,1,0:T(1,128)S(1)} all-to-all(f32[16,1,18432]{2,1,0:T(1,128)S(1)} %copy.21), channel_id=1, replica_groups=mesh['pair'=8,'sect'=4] {'pair'}, dimensions={0} | all-to-all | bytes 2359296 | tf_op jit(solution)/shard_map/all_to_all | solution.py:54
  255.6 0.7 copy.22
  256.3 1.2 reshape.21
  (11 shorter events, 0.0 us)
Async XLA Ops:
  6.5 109.4 %copy-start = (f32[2,256,1024]{2,1,0:T(8,128)S(1)}, f32[2,256,1024]{2,1,0:T(8,128)}, u32[]{:S(2)}) copy-start(f32[2,256,1024]{2,1,0:T(8,128)} %param.7) | copy-start | bytes 6291460
  6.5 78.7 %all-reduce.2.cloned.1.call-start = ((), (), s32[]{:S(2)}) async-start(), calls=%async_computation.2 | async-start | bytes 1572864 | tf_op jit(solution)/shard_map/psum | solution.py:9
  9.7 106.2 %all-gather.3.cloned.1.call-start = ((), (), s32[]{:S(2)}) async-start(), calls=%async_computation.3 | async-start | bytes 3932160 | tf_op jit(solution)/shard_map/all_gather | solution.py:22
  85.3 85.3 %all-gather.5.cloned.1.call-start = ((), (), s32[]{:S(2)}) async-start(), calls=%async_computation.4 | async-start | bytes 7864320 | tf_op jit(solution)/shard_map/all_gather | solution.py:41
  184.5 6.2 %copy-start.2 = (f32[16,16]{1,0:T(8,128)S(1)}, f32[16,16]{1,0:T(8,128)}, u32[]{:S(2)}) copy-start(f32[16,16]{1,0:T(8,128)} %param.12) | copy-start | bytes 3076
  184.5 6.2 %copy-start.3 = (s32[16]{0:T(128)S(1)}, s32[16]{0:T(128)}, u32[]{:S(2)}) copy-start(s32[16]{0:T(128)} %param.13) | copy-start | bytes 196
  184.5 6.3 %copy-start.1 = (s32[16,16]{1,0:T(8,128)S(1)}, s32[16,16]{1,0:T(8,128)}, u32[]{:S(2)}) copy-start(s32[16,16]{1,0:T(8,128)} %param.11) | copy-start | bytes 3076
  184.5 6.3 %copy-start.4 = (s32[16]{0:T(128)S(1)}, s32[16]{0:T(128)}, u32[]{:S(2)}) copy-start(s32[16]{0:T(128)} %param.10) | copy-start | bytes 196
  184.5 31.9 %all-to-all-start = ((f32[2,8,18432]{2,0,1:T(2,128)}), f32[2,8,18432]{2,0,1:T(2,128)S(1)}, u32[]{:S(2)}, u32[]{:S(2)}) async-start(f32[2,8,18432]{2,0,1:T(2,128)} %copy.20), calls=%async_computation | async-start | bytes 2359296 | tf_op jit(solution)/shard_map/all_to_all | solution.py:50
Sparse Core Ops, SparseCore 0:
  10.8 74.4 all-reduce.1
  86.9 29.0 all-gather.2
  124.2 46.3 all-gather.4
where the time goes:
time: 268 us; the launch traced here: 264 us
  waiting for transfers between devices  178 us (66%)
  blocking collectives  33.8 us (13%)
  matrix products  21 us (8%)
  between operations  14 us (5%)
  local copies, waits for them, and re-layouts  9.7 us (4%)
  starting transfers between devices  6.25 us (2%)
    psum x1, waiting for transfers between devices, broadcast(): return lax.psum(jnp.where(mine, value, jnp.zeros_like(value)), axis)  75.5 us
    all_gather x1, waiting for transfers between devices, on_device(): lax.all_gather(right_done, 'sect', axis=1, tiled=True)  46.5 us
    all_to_all x1, blocking collectives, on_device(): lax.all_to_all(mixture, 'pair', split_axis=0, concat_axis=1, tiled=True)  33.8 us
    all_gather x1, waiting for transfers between devices, on_device(): rotation_full = lax.all_gather(own_block, 'sect', axis=0, tiled=True)  30.6 us
    all_to_all x1, waiting for transfers between devices, on_device(): lax.all_to_all(blocks, 'pair', split_axis=1, concat_axis=0, tiled=True)  25.5 us
    dot_general x1, matrix products, on_device(): jnp.einsum('ia,oib->oab', columns, lax.all_gather(right_done, 'sect', axi...  10.6 us
    dot_general x1, matrix products, on_device(): jnp.einsum('oij,jb->oib', operators, rotation_full, precision=lax.Precisi...  8.09 us
    all_to_all x1, starting transfers between devices, on_device(): lax.all_to_all(blocks, 'pair', split_axis=1, concat_axis=0, tiled=True)  6.17 us
  transfers between devices with their start and end apart: 4, of which 4 were waited for; matrix products, arithmetic and copies ran while one was open for 0% of the time, Pallas kernels for 0%

commit v1 on v0

v1 whole, which is shorter than its diff:
```python
import functools

import jax
import jax.numpy as jnp
from jax import lax
from jax.experimental import pallas as pl
from jax.experimental.pallas import tpu as pltpu
from jax.sharding import PartitionSpec as P

F32, BF16 = jnp.float32, jnp.bfloat16
CHUNKS = 4


def broadcast(value, axis, root):
    mine = lax.axis_index(axis) == root
    return lax.psum(jnp.where(mine, value, jnp.zeros_like(value)), axis)


def coupling_matrix(slot_pair, sources, integrals, term_count):
    is_live = lax.broadcasted_iota(jnp.int32, sources.shape, 1) < term_count[:, None]
    weighted = jnp.where(is_live, integrals, jnp.zeros_like(integrals))
    matches = (sources[:, :, None] == slot_pair[None, None, :]).astype(jnp.float32)
    return jnp.sum(weighted[:, :, None] * matches, axis=1)


def split(value):
    high = value.astype(BF16)
    return high, (value - high.astype(F32)).astype(BF16)


def dot3(ah, al, bh, bl):
    dot = functools.partial(jnp.dot, preferred_element_type=F32)
    return dot(ah, bh) + (dot(ah, bl) + dot(al, bh))


def kernel(
    n_pair, owner_ref, coup_ref, ops_ref, rot_ref, out_ref,
    oh, ol, xbuf, cand, zr, zl, sr, sl, rfull, rh, rl, rth, rtl, rdh, rdl,
    sib_out, sib_in, own, y_out, y_in, a_out, a_in, b_out,
    x_s, x_r, zr_s, zr_r, zl_s, zl_r, px_s, px_r, py_s, py_r, pc_s, pc_r,
    c_s, c_r, y_s, y_r, a_s, a_r, b_s, b_r,
):
    local, block, width = ops_ref.shape
    wide = rot_ref.shape[1]
    half = block // 2
    chunk = half // CHUNKS
    new_rows = wide // 4
    piece = new_rows // n_pair
    depth = n_pair // 2
    p, s = lax.axis_index("pair"), lax.axis_index("sect")
    z, x = lax.div(p, 2), lax.rem(p, 2)
    y, c = lax.div(s, 2), lax.rem(s, 2)

    def dev(pp, ss):
        return {"pair": pp, "sect": ss}

    x_nb = dev(p + 1 - 2 * x, s)
    y_nb = dev(p, s + 2 - 4 * y)
    c_nb = dev(p, s + 1 - 2 * c)
    z_up, z_dn = dev(p + 2, s), dev(p - 2, s)

    def copy(src, dst, ssem, rsem, device):
        return pltpu.make_async_remote_copy(
            src_ref=src, dst_ref=dst, send_sem=ssem, recv_sem=rsem,
            device_id=device, device_id_type=pl.DeviceIdType.MESH,
        )

    def rows(start, size, step=8):
        if not isinstance(start, int):
            start = pl.multiple_of(start, step)
        return pl.ds(start, size)

    barrier = pltpu.get_barrier_semaphore()
    for m in range(1, n_pair):
        pl.semaphore_signal(barrier, inc=1, device_id=dev(lax.rem(p + m, n_pair), s),
                            device_id_type=pl.DeviceIdType.MESH)
    for nb in (y_nb, c_nb):
        pl.semaphore_signal(barrier, inc=1, device_id=nb, device_id_type=pl.DeviceIdType.MESH)

    @pl.when(z == 0)
    def _():
        zr[...] = jnp.zeros_like(zr)

    @pl.when(z == depth - 1)
    def _():
        zl[...] = jnp.zeros_like(zl)

    pl.semaphore_wait(barrier, n_pair + 1)

    def x_copy(k):
        return copy(rot_ref.at[rows((1 - x) * half + k * chunk, chunk)],
                    xbuf.at[rows(k * chunk, chunk)], x_s.at[k], x_r.at[k], x_nb)

    for k in range(CHUNKS):
        x_copy(k).start()

    for g in range(local):
        for r in range(2):
            at = pl.ds(r * half, half)
            to = pl.ds(g * block + r * half, half)
            oh[to], ol[to] = split(ops_ref[g, at])

    owner = owner_ref[0]
    owner_z, owner_x = lax.div(owner, 2), lax.rem(owner, 2)

    def r_copy(k):
        at = rows(k * chunk, chunk)
        return copy(sr.at[at], zr.at[at], zr_s.at[k], zr_r.at[k], z_up)

    def l_copy(k):
        at = rows(k * chunk, chunk)
        return copy(sl.at[at], zl.at[at], zl_s.at[k], zl_r.at[k], z_dn)

    def place(yy, cc, xx, k):
        return rows((yy * 2 + cc) * block + xx * half + k * chunk, chunk)

    def p_copy(at, sends, recvs, i, device):
        return copy(rfull.at[at], rfull.at[at], sends.at[i], recvs.at[i], device)

    def refine(yy, cc, xx):
        at = rows((yy * 2 + cc) * block + xx * half, half, 16)
        rh[at], rl[at] = split(rfull[at])

    far = jnp.maximum(z, depth - 1 - z)
    for t in range(CHUNKS + depth - 1):
        if t < CHUNKS:
            x_copy(t).wait_recv()
            at = rows(t * chunk, chunk)
            mine = rot_ref[rows(x * half + t * chunk, chunk)]
            cand[at] = jnp.where(owner_x == x, mine, xbuf[at])
        kr, kl, kf = t - z, t - (depth - 1 - z), t - far

        @pl.when((kr >= 0) & (kr < CHUNKS))
        def _():
            at = rows(kr * chunk, chunk)

            @pl.when(z > 0)
            def _():
                r_copy(kr).wait_recv()

            @pl.when(z < depth - 1)
            def _():
                sr[at] = jnp.where(owner_z == z, cand[at], zr[at])
                r_copy(kr).start()

        @pl.when((kl >= 0) & (kl < CHUNKS))
        def _():
            at = rows(kl * chunk, chunk)

            @pl.when(z < depth - 1)
            def _():
                l_copy(kl).wait_recv()

            @pl.when(z > 0)
            def _():
                sl[at] = jnp.where(owner_z == z, cand[at], zl[at])
                l_copy(kl).start()

        @pl.when((kf >= 0) & (kf < CHUNKS))
        def _():
            at = rows(kf * chunk, chunk)
            to = place(y, c, x, kf)
            rfull[to] = jnp.where(owner_z == z, cand[at], jnp.where(owner_z < z, zr[at], zl[at]))
            p_copy(to, px_s, px_r, kf, x_nb).start()
            p_copy(to, py_s, py_r, kf, y_nb).start()
            p_copy(to, pc_s, pc_r, kf, c_nb).start()

    refine(y, c, x)
    for k in range(CHUNKS):
        at = place(y, c, 1 - x, k)
        p_copy(at, px_s, px_r, k, x_nb).wait_recv()
        if k % 2 == 0:
            p_copy(at, py_s, py_r, CHUNKS + k // 2, y_nb).start()
        p_copy(at, pc_s, pc_r, CHUNKS + k, c_nb).start()
        at = place(1 - y, c, x, k)
        p_copy(at, py_s, py_r, k, y_nb).wait_recv()
        if k % 2 == 1:
            p_copy(at, px_s, px_r, CHUNKS + k // 2, x_nb).start()
        p_copy(at, pc_s, pc_r, 2 * CHUNKS + k, c_nb).start()
    refine(y, c, 1 - x)
    refine(1 - y, c, x)
    turned = rfull[rows(s * block, block)].T
    rth[...], rtl[...] = split(turned)
    for k in range(CHUNKS):
        at = place(1 - y, c, 1 - x, k)
        if k % 2 == 0:
            p_copy(at, py_s, py_r, CHUNKS + k // 2, y_nb).wait_recv()
        else:
            p_copy(at, px_s, px_r, CHUNKS + k // 2, x_nb).wait_recv()
        p_copy(at, pc_s, pc_r, 3 * CHUNKS + k, c_nb).start()
    refine(1 - y, c, 1 - x)
    others = ((y, x), (y, 1 - x), (1 - y, x), (1 - y, 1 - x))
    for i, (yy, xx) in enumerate(others):
        for k in range(CHUNKS):
            p_copy(place(yy, 1 - c, xx, k), pc_s, pc_r, i * CHUNKS + k, c_nb).wait_recv()
        refine(yy, 1 - c, xx)

    tile = 256 if wide % 256 == 0 else wide
    for n in range(wide // tile):
        at = pl.ds(n * tile, tile)
        done = dot3(oh[...], ol[...], rh[:, at], rl[:, at])
        rdh[:, at], rdl[:, at] = split(done)

    def partial(yy, cc, g):
        at = rows((yy * 2 + cc) * new_rows, new_rows, 16)
        on = pl.ds(g * block, block)
        return dot3(rth[at], rtl[at], rdh[on], rdl[on])

    def c_copy(i, g):
        return copy(sib_out.at[i, g], sib_in.at[i, g], c_s.at[i * local + g], c_r.at[i * local + g], c_nb)

    sides = (1 - y, y)
    for i in range(2):
        for g in range(local):
            sib_out[i, g] = partial(sides[i], 1 - c, g)
            c_copy(i, g).start()
    for g in range(local):
        own[0, g] = partial(sides[0], c, g)

    steps = sorted(range(n_pair), key=lambda m: (-min(m, n_pair - m), m))

    def y_copy(m):
        return copy(y_out.at[m], y_in.at[m], y_s.at[m], y_r.at[m], y_nb)

    for g in range(local):
        c_copy(0, g).wait_recv()
    for m in steps:
        at = rows(lax.rem(p + m, n_pair) * piece, piece)
        y_out[m] = own[0, :, at] + sib_in[0, :, at]
        y_copy(m).start()
    for g in range(local):
        own[1, g] = partial(sides[1], c, g)
        c_copy(1, g).wait_recv()

    def a_copy(m, slot):
        return copy(a_out.at[m], a_in.at[slot], a_s.at[m], a_r.at[m], dev(lax.rem(p + m, n_pair), s))

    for m in steps:
        at = rows(lax.rem(p + m, n_pair) * piece, piece)
        y_copy(m).wait_recv()
        total = own[1, :, at] + sib_in[1, :, at] + y_in[m]
        if m == 0:
            a_in[p] = total
        else:
            a_out[m] = total
            a_copy(m, p).start()
    for m in range(1, n_pair):
        a_copy(m, lax.rem(p - m + n_pair, n_pair)).wait_recv()

    def b_copy(m, slot):
        return copy(b_out.at[m], out_ref.at[:, rows(slot * piece, piece)], b_s.at[m], b_r.at[m],
                    dev(lax.rem(p + m, n_pair), s))

    for m in steps:
        q = lax.rem(p + m, n_pair)
        for j in range(local):
            total = None
            for g in range(n_pair * local):
                term = coup_ref[q * local + j, g] * a_in[g // local, g % local]
                total = term if total is None else total + term
            if m == 0:
                out_ref[j, rows(p * piece, piece)] = total
            else:
                b_out[m, j] = total
        if m:
            b_copy(m, p).start()
    for m in range(1, n_pair):
        b_copy(m, lax.rem(p - m + n_pair, n_pair)).wait_recv()

    for k in range(CHUNKS):
        x_copy(k).wait_send()

        @pl.when(z < depth - 1)
        def _():
            r_copy(k).wait_send()

        @pl.when(z > 0)
        def _():
            l_copy(k).wait_send()

    first = place(y, c, x, 0)
    for i in range(CHUNKS + CHUNKS // 2):
        p_copy(first, px_s, px_r, i, x_nb).wait_send()
        p_copy(first, py_s, py_r, i, y_nb).wait_send()
    for i in range(4 * CHUNKS):
        p_copy(first, pc_s, pc_r, i, c_nb).wait_send()
    for i in range(2):
        for g in range(local):
            c_copy(i, g).wait_send()
    for m in range(n_pair):
        y_copy(m).wait_send()
        if m:
            a_copy(m, p).wait_send()
            b_copy(m, p).wait_send()


def fused(operators, rotation, owner, coupling, n_pair):
    local, block, width = operators.shape
    wide = rotation.shape[1]
    half, new_rows = block // 2, wide // 4
    piece = new_rows // n_pair
    dma = pltpu.SemaphoreType.DMA
    vmem = pltpu.VMEM
    chain = [vmem((half, wide), F32)] * 6
    scratch = [vmem((local * block, width), BF16)] * 2 + chain + [
        vmem((width, wide), F32),
        vmem((width, wide), BF16), vmem((width, wide), BF16),
        vmem((wide, block), BF16), vmem((wide, block), BF16),
        vmem((local * block, wide), BF16), vmem((local * block, wide), BF16),
        vmem((2, local, new_rows, wide), F32),
        vmem((2, local, new_rows, wide), F32),
        vmem((2, local, new_rows, wide), F32),
        vmem((n_pair, local, piece, wide), F32),
        vmem((n_pair, local, piece, wide), F32),
        vmem((n_pair, local, piece, wide), F32),
        vmem((n_pair, local, piece, wide), F32),
        vmem((n_pair, local, piece, wide), F32),
    ]
    links = CHUNKS + CHUNKS // 2
    counts = [CHUNKS] * 6 + [links] * 4 + [4 * CHUNKS] * 2 + [2 * local] * 2 + [n_pair] * 6
    scratch += [dma((count,)) for count in counts]
    smem = pl.BlockSpec(memory_space=pltpu.SMEM)
    in_vmem = pl.BlockSpec(memory_space=pltpu.VMEM)
    return pl.pallas_call(
        functools.partial(kernel, n_pair),
        out_shape=jax.ShapeDtypeStruct((local, new_rows, wide), F32),
        in_specs=[smem, smem, in_vmem, in_vmem],
        out_specs=in_vmem,
        scratch_shapes=scratch,
        compiler_params=pltpu.CompilerParams(
            collective_id=0, has_side_effects=True, vmem_limit_bytes=56 * 1024 * 1024
        ),
    )(owner, coupling, operators, rotation)


def on_device(fits, operators, rotations, sector_owner, slot_pair, sources, integrals, term_count):
    sect_count = lax.axis_size("sect")
    pair_count = lax.axis_size("pair")
    local_ops = operators.shape[0]
    coupling = coupling_matrix(slot_pair, sources, integrals, term_count)
    if fits:
        return fused(operators, rotations[0], sector_owner, coupling, pair_count)
    own_block = broadcast(rotations[0], "pair", sector_owner[0])
    rotation_full = lax.all_gather(own_block, "sect", axis=0, tiled=True)
    width_new = rotation_full.shape[1]
    new_rows = width_new // sect_count
    highest = dict(precision=lax.Precision.HIGHEST, preferred_element_type=jnp.float32)
    right_done = jnp.einsum("oij,jb->oib", operators, rotation_full, **highest)
    columns = lax.dynamic_slice_in_dim(
        rotation_full, lax.axis_index("sect") * new_rows, new_rows, 1
    )
    rotated = jnp.einsum(
        "ia,oib->oab",
        columns,
        lax.all_gather(right_done, "sect", axis=1, tiled=True),
        **highest,
    )
    blocks = rotated.reshape(local_ops, pair_count, -1)
    mixture = jnp.einsum(
        "or,rhn->ohn",
        coupling,
        lax.all_to_all(blocks, "pair", split_axis=1, concat_axis=0, tiled=True),
        **highest,
    )
    result = lax.all_to_all(mixture, "pair", split_axis=0, concat_axis=1, tiled=True)
    return result.reshape(local_ops, new_rows, width_new)


def solution(mesh):
    pair_count, sect_count = mesh.shape["pair"], mesh.shape["sect"]

    def call(operators, rotations, *rest):
        wide = rotations.shape[2]
        fits = sect_count == 4 and pair_count % 2 == 0 and wide % (8 * pair_count * sect_count) == 0
        in_specs = (P("pair", "sect", None), P("pair", "sect", None), P(), P(), P(), P(), P())
        return jax.shard_map(
            functools.partial(on_device, fits), mesh=mesh, in_specs=in_specs,
            out_specs=P("pair", "sect", None), check_vma=False,
        )(operators, rotations, *rest)

    return call
```

time: 268 us -> 111 us (0.41); the launches traced: 264 us -> 110 us
  waiting for transfers between devices: 178 us -> 0 us
  Pallas kernels: 0 us -> 105 us
  blocking collectives: 33.8 us -> 0 us
  matrix products: 21 us -> 0 us
  between operations: 14 us -> 0.66 us
  local copies, waits for them, and re-layouts: 9.7 us -> 2.36 us
  starting transfers between devices: 6.25 us -> 0 us
    pallas_call x0 -> x1, Pallas kernels: none -> 105 us  [fused(): pl.pallas_call(functools.partial(kernel, n_pair), out_shape=jax.ShapeDtyp...]
    all_gather x2 -> x0, waiting for transfers between devices: 77.2 us -> none  [the longest x1 46.5 us: on_device(): lax.all_gather(right_done, 'sect', axis=1, tiled=True)]
    psum x1 -> x0, waiting for transfers between devices: 75.5 us -> none  [broadcast(): return lax.psum(jnp.where(mine, value, jnp.zeros_like(value)), axis)]
    all_to_all x1 -> x0, blocking collectives: 33.8 us -> none  [on_device(): lax.all_to_all(mixture, 'pair', split_axis=0, concat_axis=1, tiled=True)]
    all_to_all x1 -> x0, waiting for transfers between devices: 25.5 us -> none  [on_device(): lax.all_to_all(blocks, 'pair', split_axis=1, concat_axis=0, tiled=True)]
    dot_general x3 -> x0, matrix products: 21 us -> none  [the longest x1 10.6 us: on_device(): jnp.einsum('ia,oib->oab', columns, lax.all_gather(right_done, 'sect', axi...]
    reshape x4 -> x0, local copies, waits for them, and re-layouts: 6.39 us -> none  [the longest x2 3.37 us: on_device(): blocks = rotated.reshape(local_ops, pair_count, -1)]
    all_to_all x1 -> x0, starting transfers between devices: 6.17 us -> none  [on_device(): lax.all_to_all(blocks, 'pair', split_axis=1, concat_axis=0, tiled=True)]
  transfers between devices with their start and end apart: 4 -> 0, of which waited for: 4 -> 0; matrix products, arithmetic and copies ran while one was open for 0% -> 0% of each run, Pallas kernels for 0% -> 0%
where the time goes in v1:
time: 111 us; the launch traced here: 110 us
  Pallas kernels  105 us (95%)
  local copies, waits for them, and re-layouts  2.36 us (2%)
  other arithmetic  2.23 us (2%)
    pallas_call x1, Pallas kernels, fused(): pl.pallas_call(functools.partial(kernel, n_pair), out_shape=jax.ShapeDtyp...  105 us
    unnamed x1, local copies, waits for them, and re-layouts  2.36 us

profile of v1, /device:TPU:16, one launch (start us, length us, event | category | flops | bytes accessed | tf_op | source)
XLA Modules:
  0.0 110.2 jit_solution(13920445735452476034)
XLA Ops:
  0.7 0.8 fusion
  1.4 1.5 %select_reduce_fusion.coup_ref = f32[16,16]{1,0:T(8,128)} fusion(f32[16,16]{1,0:T(8,128)S(1)} %fusion, s32[16]{0:T(128)} %param.10, s32[16,16]{1,0:T(8,128)} %param.11), kind=kLoop, calls=%fused_computation | loop fusion | flops 12032 | bytes 3136 | tf_op jit(solution)/shard_map/reduce_sum | solution.py:23
  2.9 105.0 %shard_map.73 = f32[2,192,768]{2,1,0:T(8,128)} custom-call(s32[1]{0:T(128)S(6)} %copy.9.owner_ref, f32[16,16]{1,0:T(8,128)} %select_reduce_fusion.coup_ref, f32[2,256,1024]{2,1,0:T(8,128)} %ops_ref.1, f32[256,768]{1,0:T(8,128)} %bitcast.1), custom_call_target="tpu_custom_call" | custom-call | tf_op jit(solution)/shard_map/pallas_call | solution.py:324
  107.9 2.4 %copy.10 = f32[2,192,768]{2,1,0:T(8,128)} copy(f32[2,192,768]{2,1,0:T(8,128)} %shard_map.73) | data formatting | bytes 2359296

commit v2 on v1

--- a/solution.py
+++ b/solution.py
@@ -34,14 +34,14 @@
 
 
 def kernel(
-    n_pair, owner_ref, coup_ref, ops_ref, rot_ref, out_ref,
-    oh, ol, xbuf, cand, zr, zl, sr, sl, rfull, rh, rl, rth, rtl, rdh, rdl,
+    n_pair, owner_ref, slot_ref, count_ref, sources_ref, integrals_ref, ops_in, rot_in, out_ref,
+    ops_ref, rot_ref, table, load_sem, oh, ol, xbuf, cand, zr, zl, sr, sl, rfull, rh, rl, rth, rtl, rdh, rdl,
     sib_out, sib_in, own, y_out, y_in, a_out, a_in, b_out,
     x_s, x_r, zr_s, zr_r, zl_s, zl_r, px_s, px_r, py_s, py_r, pc_s, pc_r,
     c_s, c_r, y_s, y_r, a_s, a_r, b_s, b_r,
 ):
-    local, block, width = ops_ref.shape
-    wide = rot_ref.shape[1]
+    local, block, width = ops_in.shape
+    wide = rot_in.shape[1]
     half = block // 2
     chunk = half // CHUNKS
     new_rows = wide // 4
@@ -70,6 +70,10 @@
             start = pl.multiple_of(start, step)
         return pl.ds(start, size)
 
+    load_ops = pltpu.make_async_copy(ops_in, ops_ref, load_sem.at[0])
+    load_rot = pltpu.make_async_copy(rot_in, rot_ref, load_sem.at[1])
+    load_rot.start()
+    load_ops.start()
     barrier = pltpu.get_barrier_semaphore()
     for m in range(1, n_pair):
         pl.semaphore_signal(barrier, inc=1, device_id=dev(lax.rem(p + m, n_pair), s),
@@ -85,6 +89,7 @@
     def _():
         zl[...] = jnp.zeros_like(zl)
 
+    load_rot.wait()
     pl.semaphore_wait(barrier, n_pair + 1)
 
     def x_copy(k):
@@ -94,11 +99,23 @@
     for k in range(CHUNKS):
         x_copy(k).start()
 
+    load_ops.wait()
     for g in range(local):
         for r in range(2):
             at = pl.ds(r * half, half)
             to = pl.ds(g * block + r * half, half)
             oh[to], ol[to] = split(ops_ref[g, at])
+
+    n_ops = sources_ref.shape[0]
+    row = lax.broadcasted_iota(jnp.int32, sources_ref.shape, 0)
+    entry = lax.broadcasted_iota(jnp.int32, sources_ref.shape, 1)
+    live = jnp.zeros(sources_ref.shape, jnp.int32)
+    for j in range(n_ops):
+        live = jnp.where(row == j, count_ref[j], live)
+    weighted = jnp.where(entry < live, integrals_ref[...], 0.0)
+    for g in range(n_ops):
+        hit = jnp.where(sources_ref[...] == slot_ref[g], weighted, 0.0)
+        table[g] = jnp.broadcast_to(jnp.sum(hit, axis=1, keepdims=True), (n_ops, 128))
 
     owner = owner_ref[0]
     owner_z, owner_x = lax.div(owner, 2), lax.rem(owner, 2)
@@ -253,15 +270,17 @@
 
     for m in steps:
         q = lax.rem(p + m, n_pair)
-        for j in range(local):
-            total = None
-            for g in range(n_pair * local):
-                term = coup_ref[q * local + j, g] * a_in[g // local, g % local]
-                total = term if total is None else total + term
-            if m == 0:
-                out_ref[j, rows(p * piece, piece)] = total
-            else:
-                b_out[m, j] = total
+        for n in range(wide // 128):
+            at = pl.ds(n * 128, 128)
+            for j in range(local):
+                total = None
+                for g in range(n_ops):
+                    term = table[g, pl.ds(q * local + j, 1)] * a_in[g // local, g % local, :, at]
+                    total = term if total is None else total + term
+                if m == 0:
+                    out_ref[j, rows(p * piece, piece), at] = total
+                else:
+                    b_out[m, j, :, at] = total
         if m:
             b_copy(m, p).start()
     for m in range(1, n_pair):
@@ -294,7 +313,7 @@
             b_copy(m, p).wait_send()
 
 
-def fused(operators, rotation, owner, coupling, n_pair):
+def fused(operators, rotation, owner, slot_pair, term_count, sources, integrals, n_pair):
     local, block, width = operators.shape
     wide = rotation.shape[1]
     half, new_rows = block // 2, wide // 4
@@ -302,7 +321,9 @@
     dma = pltpu.SemaphoreType.DMA
     vmem = pltpu.VMEM
     chain = [vmem((half, wide), F32)] * 6
-    scratch = [vmem((local * block, width), BF16)] * 2 + chain + [
+    scratch = [vmem((local, block, width), F32), vmem((block, wide), F32),
+               vmem((local * n_pair, local * n_pair, 128), F32), dma((2,))]
+    scratch += [vmem((local * block, width), BF16)] * 2 + chain + [
         vmem((width, wide), F32),
         vmem((width, wide), BF16), vmem((width, wide), BF16),
         vmem((wide, block), BF16), vmem((wide, block), BF16),
@@ -323,23 +344,24 @@
     in_vmem = pl.BlockSpec(memory_space=pltpu.VMEM)
     return pl.pallas_call(
         functools.partial(kernel, n_pair),
-        out_shape=jax.ShapeDtypeStruct((local, new_rows, wide), F32),
-        in_specs=[smem, smem, in_vmem, in_vmem],
+        out_shape=pltpu.VMEM((local, new_rows, wide), F32),
+        in_specs=[smem] * 3 + [in_vmem] * 2 + [pl.BlockSpec(memory_space=pl.ANY)] * 2,
         out_specs=in_vmem,
         scratch_shapes=scratch,
         compiler_params=pltpu.CompilerParams(
             collective_id=0, has_side_effects=True, vmem_limit_bytes=56 * 1024 * 1024
         ),
-    )(owner, coupling, operators, rotation)
+    )(owner, slot_pair, term_count, sources, integrals, operators, rotation)
 
 
 def on_device(fits, operators, rotations, sector_owner, slot_pair, sources, integrals, term_count):
     sect_count = lax.axis_size("sect")
     pair_count = lax.axis_size("pair")
     local_ops = operators.shape[0]
+    if fits:
+        return fused(operators, rotations[0], sector_owner, slot_pair, term_count,
+                     sources, integrals, pair_count)
     coupling = coupling_matrix(slot_pair, sources, integrals, term_count)
-    if fits:
-        return fused(operators, rotations[0], sector_owner, coupling, pair_count)
     own_block = broadcast(rotations[0], "pair", sector_owner[0])
     rotation_full = lax.all_gather(own_block, "sect", axis=0, tiled=True)
     width_new = rotation_full.shape[1]

time: 111 us -> 105 us (0.946)
  other arithmetic: 2.23 us -> 0 us
  Pallas kernels: 105 us -> 103 us
  local copies, waits for them, and re-layouts: 2.36 us -> 1.02 us
    pallas_call x1, Pallas kernels: 105 us -> 103 us  [fused(): pl.pallas_call(functools.partial(kernel, n_pair), out_shape=pltpu.VMEM((l...]
    reduce_sum x1 -> x0, other arithmetic: 1.46 us -> none  [coupling_matrix(): return jnp.sum(weighted[:, :, None] * matches, axis=1)]
    unnamed x1, local copies, waits for them, and re-layouts: 2.36 us -> 1.02 us
where the time goes in v2:
time: 105 us
  Pallas kernels  103 us (98%)
    pallas_call x1, Pallas kernels, fused(): pl.pallas_call(functools.partial(kernel, n_pair), out_shape=pltpu.VMEM((l...  103 us

profile of v2, /device:TPU:16, one launch (start us, length us, event | category | flops | bytes accessed | tf_op | source)
XLA Modules:
  0.0 104.7 jit_solution(6062772165542662715)
XLA Ops:
  0.7 103.0 %shard_map.73 = f32[2,192,768]{2,1,0:T(8,128)S(1)} custom-call(s32[1]{0:T(128)S(6)} %copy.10.owner_ref, s32[16]{0:T(128)} %slot_ref.1, s32[16]{0:T(128)} %count_ref.1, s32[16,16]{1,0:T(8,128)} %sources_ref.1, f32[16,16]{1,0:T(8,128)} %integrals_ref.1, f32[2,256,1024]{2,1,0:T(8,128)} %ops_in.1, f32[256,768]{1,0:T(8,128)} %bitcast.1), custom_call_target="tpu_custom_call" | custom-call | tf_op jit(solution)/shard_map/pallas_call | solution.py:345
  103.7 1.0 copy.9

commit v3 on v2

v3 whole, which is shorter than its diff:
```python
import functools

import jax
import jax.numpy as jnp
from jax import lax
from jax.experimental import pallas as pl
from jax.experimental.pallas import tpu as pltpu
from jax.sharding import PartitionSpec as P

F32, BF16 = jnp.float32, jnp.bfloat16
CHUNKS = 4
LAG = 2
PARTS = 2


def broadcast(value, axis, root):
    mine = lax.axis_index(axis) == root
    return lax.psum(jnp.where(mine, value, jnp.zeros_like(value)), axis)


def coupling_matrix(slot_pair, sources, integrals, term_count):
    is_live = lax.broadcasted_iota(jnp.int32, sources.shape, 1) < term_count[:, None]
    weighted = jnp.where(is_live, integrals, jnp.zeros_like(integrals))
    matches = (sources[:, :, None] == slot_pair[None, None, :]).astype(jnp.float32)
    return jnp.sum(weighted[:, :, None] * matches, axis=1)


def split(value):
    high = value.astype(BF16)
    return high, (value - high.astype(F32)).astype(BF16)


def dot3(ah, al, bh, bl):
    dot = functools.partial(jnp.dot, preferred_element_type=F32)
    return dot(ah, bh) + (dot(ah, bl) + dot(al, bh))


def kernel(
    n_pair, owner_ref, slot_ref, count_ref, sources_ref, integrals_ref, ops_in, rot_in, out_ref,
    ops_ref, rot_ref, table, load_sem, oh, ol, xbuf, cand, zr, zl, sr, sl, rfull, rh, rl, rth, rtl, rdh, rdl,
    sib_out, sib_in, own, y_out, y_in, a_out, a_in, b_out,
    x_s, x_r, zr_s, zr_r, zl_s, zl_r, px_s, px_r, py_s, py_r, pc_s, pc_r,
    c_s, c_r, y_s, y_r, a_s, a_r, b_s, b_r,
):
    local, block, width = ops_in.shape
    wide = rot_in.shape[1]
    half = block // 2
    chunk = half // CHUNKS
    new_rows = wide // 4
    piece = new_rows // n_pair
    depth = n_pair // 2
    p, s = lax.axis_index("pair"), lax.axis_index("sect")
    z, x = lax.div(p, 2), lax.rem(p, 2)
    y, c = lax.div(s, 2), lax.rem(s, 2)

    def dev(pp, ss):
        return {"pair": pp, "sect": ss}

    x_nb = dev(p + 1 - 2 * x, s)
    y_nb = dev(p, s + 2 - 4 * y)
    c_nb = dev(p, s + 1 - 2 * c)
    z_up, z_dn = dev(p + 2, s), dev(p - 2, s)

    def copy(src, dst, ssem, rsem, device):
        return pltpu.make_async_remote_copy(
            src_ref=src, dst_ref=dst, send_sem=ssem, recv_sem=rsem,
            device_id=device, device_id_type=pl.DeviceIdType.MESH,
        )

    def rows(start, size, step=8):
        if not isinstance(start, int):
            start = pl.multiple_of(start, step)
        return pl.ds(start, size)

    load_ops = pltpu.make_async_copy(ops_in, ops_ref, load_sem.at[0])
    load_rot = pltpu.make_async_copy(rot_in, rot_ref, load_sem.at[1])
    load_rot.start()
    load_ops.start()
    barrier = pltpu.get_barrier_semaphore()
    for m in range(1, n_pair):
        pl.semaphore_signal(barrier, inc=1, device_id=dev(lax.rem(p + m, n_pair), s),
                            device_id_type=pl.DeviceIdType.MESH)
    for nb in (y_nb, c_nb):
        pl.semaphore_signal(barrier, inc=1, device_id=nb, device_id_type=pl.DeviceIdType.MESH)

    @pl.when(z == 0)
    def _():
        zr[...] = jnp.zeros_like(zr)

    @pl.when(z == depth - 1)
    def _():
        zl[...] = jnp.zeros_like(zl)

    load_rot.wait()
    pl.semaphore_wait(barrier, n_pair + 1)

    def x_copy(k):
        return copy(rot_ref.at[rows((1 - x) * half + k * chunk, chunk)],
                    xbuf.at[rows(k * chunk, chunk)], x_s.at[k], x_r.at[k], x_nb)

    for k in range(CHUNKS):
        x_copy(k).start()

    load_ops.wait()
    for g in range(local):
        for r in range(2):
            at = pl.ds(r * half, half)
            to = pl.ds(g * block + r * half, half)
            oh[to], ol[to] = split(ops_ref[g, at])

    owner = owner_ref[0]
    owner_z, owner_x = lax.div(owner, 2), lax.rem(owner, 2)

    def r_copy(k):
        at = rows(k * chunk, chunk)
        return copy(sr.at[at], zr.at[at], zr_s.at[k], zr_r.at[k], z_up)

    def l_copy(k):
        at = rows(k * chunk, chunk)
        return copy(sl.at[at], zl.at[at], zl_s.at[k], zl_r.at[k], z_dn)

    def place(yy, cc, xx, k):
        return rows((yy * 2 + cc) * block + xx * half + k * chunk, chunk)

    def p_copy(at, sends, recvs, i, device):
        return copy(rfull.at[at], rfull.at[at], sends.at[i], recvs.at[i], device)

    def core_copy(i, xx, yy, cc, k):
        at = rows((yy * 2 + cc) * block + xx * half + k * chunk, 2 * chunk)
        index = i * (CHUNKS // 2) + (k // 2 if isinstance(k, int) else lax.div(k, 2))
        return p_copy(at, pc_s, pc_r, index, c_nb)

    def refine(yy, cc, xx):
        at = rows((yy * 2 + cc) * block + xx * half, half, 16)
        rh[at], rl[at] = split(rfull[at])

    far = jnp.maximum(z, depth - 1 - z)
    for t in range(CHUNKS + depth - 1 + LAG):
        if t < CHUNKS:
            x_copy(t).wait_recv()
            at = rows(t * chunk, chunk)
            mine = rot_ref[rows(x * half + t * chunk, chunk)]
            cand[at] = jnp.where(owner_x == x, mine, xbuf[at])
        kr, kl, kf = t - z, t - (depth - 1 - z), t - far

        @pl.when((kr >= 0) & (kr < CHUNKS))
        def _():
            at = rows(kr * chunk, chunk)

            @pl.when(z > 0)
            def _():
                r_copy(kr).wait_recv()

            @pl.when(z < depth - 1)
            def _():
                sr[at] = jnp.where(owner_z == z, cand[at], zr[at])
                r_copy(kr).start()

        @pl.when((kl >= 0) & (kl < CHUNKS))
        def _():
            at = rows(kl * chunk, chunk)

            @pl.when(z < depth - 1)
            def _():
                l_copy(kl).wait_recv()

            @pl.when(z > 0)
            def _():
                sl[at] = jnp.where(owner_z == z, cand[at], zl[at])
                l_copy(kl).start()

        kg = kf - LAG

        @pl.when((kf >= 0) & (kf < CHUNKS))
        def _():
            at = rows(kf * chunk, chunk)
            to = place(y, c, x, kf)
            rfull[to] = jnp.where(owner_z == z, cand[at], jnp.where(owner_z < z, zr[at], zl[at]))
            p_copy(to, px_s, px_r, kf, x_nb).start()
            p_copy(to, py_s, py_r, kf, y_nb).start()

            @pl.when(lax.rem(kf, 2) == 1)
            def _():
                core_copy(0, x, y, c, kf - 1).start()

        @pl.when((kg >= 0) & (kg < CHUNKS))
        def _():
            from_x, from_y = place(y, c, 1 - x, kg), place(1 - y, c, x, kg)
            p_copy(from_x, px_s, px_r, kg, x_nb).wait_recv()
            p_copy(from_y, py_s, py_r, kg, y_nb).wait_recv()
            onward = CHUNKS + lax.div(kg, 2)

            @pl.when(lax.rem(kg, 2) == 0)
            def _():
                p_copy(from_x, py_s, py_r, onward, y_nb).start()

            @pl.when(lax.rem(kg, 2) == 1)
            def _():
                p_copy(from_y, px_s, px_r, onward, x_nb).start()
                core_copy(1, 1 - x, y, c, kg - 1).start()
                core_copy(2, x, 1 - y, c, kg - 1).start()

    refine(y, c, x)
    for k in range(CHUNKS):
        at = place(1 - y, c, 1 - x, k)
        if k % 2 == 0:
            p_copy(at, py_s, py_r, CHUNKS + k // 2, y_nb).wait_recv()
        else:
            p_copy(at, px_s, px_r, CHUNKS + k // 2, x_nb).wait_recv()
            core_copy(3, 1 - x, 1 - y, c, k - 1).start()
    refine(y, c, 1 - x)
    refine(1 - y, c, x)
    refine(1 - y, c, 1 - x)
    turned = rfull[rows(s * block, block)].T
    rth[...], rtl[...] = split(turned)
    others = ((y, x), (y, 1 - x), (1 - y, x), (1 - y, 1 - x))
    for i, (yy, xx) in enumerate(others):
        for k in range(0, CHUNKS, 2):
            core_copy(i, xx, yy, 1 - c, k).wait_recv()
        refine(yy, 1 - c, xx)

    tile = 256 if wide % 256 == 0 else wide
    for n in range(wide // tile):
        at = pl.ds(n * tile, tile)
        done = dot3(oh[...], ol[...], rh[:, at], rl[:, at])
        rdh[:, at], rdl[:, at] = split(done)

    def partial(yy, cc, g):
        at = rows((yy * 2 + cc) * new_rows, new_rows, 16)
        on = pl.ds(g * block, block)
        return dot3(rth[at], rtl[at], rdh[on], rdl[on])

    def c_copy(i, g):
        return copy(sib_out.at[i, g], sib_in.at[i, g], c_s.at[i * local + g], c_r.at[i * local + g], c_nb)

    sides = (1 - y, y)
    for i in range(2):
        for g in range(local):
            sib_out[i, g] = partial(sides[i], 1 - c, g)
            c_copy(i, g).start()
    for g in range(local):
        own[0, g] = partial(sides[0], c, g)

    steps = sorted(range(n_pair), key=lambda m: (-min(m, n_pair - m), m))

    def columns(u):
        return pl.ds(u * (wide // PARTS), wide // PARTS)

    def y_copy(m, u):
        at, i = columns(u), u * n_pair + m
        return copy(y_out.at[m, :, :, at], y_in.at[m, :, :, at], y_s.at[i], y_r.at[i], y_nb)

    turns = [(u, m) for u in range(PARTS) for m in steps]
    turns_away = [(u, m) for u, m in turns if m]

    for g in range(local):
        c_copy(0, g).wait_recv()
    for u, m in turns:
        at, on = rows(lax.rem(p + m, n_pair) * piece, piece), columns(u)
        y_out[m, :, :, on] = own[0, :, at, on] + sib_in[0, :, at, on]
        y_copy(m, u).start()
    for g in range(local):
        own[1, g] = partial(sides[1], c, g)
        c_copy(1, g).wait_recv()

    def a_copy(m, u, slot):
        at, i = columns(u), u * n_pair + m
        return copy(a_out.at[m, :, :, at], a_in.at[slot, :, :, at], a_s.at[i], a_r.at[i],
                    dev(lax.rem(p + m, n_pair), s))

    for u, m in turns:
        at, on = rows(lax.rem(p + m, n_pair) * piece, piece), columns(u)
        y_copy(m, u).wait_recv()
        total = own[1, :, at, on] + sib_in[1, :, at, on] + y_in[m, :, :, on]
        if m == 0:
            a_in[p, :, :, on] = total
        else:
            a_out[m, :, :, on] = total
            a_copy(m, u, p).start()

    for k in range(CHUNKS):
        x_copy(k).wait_send()

        @pl.when(z < depth - 1)
        def _():
            r_copy(k).wait_send()

        @pl.when(z > 0)
        def _():
            l_copy(k).wait_send()

    first = place(y, c, x, 0)
    for i in range(CHUNKS + CHUNKS // 2):
        p_copy(first, px_s, px_r, i, x_nb).wait_send()
        p_copy(first, py_s, py_r, i, y_nb).wait_send()
    for i in range(4):
        for k in range(0, CHUNKS, 2):
            core_copy(i, x, y, c, k).wait_send()
    for i in range(2):
        for g in range(local):
            c_copy(i, g).wait_send()
    for u, m in turns:
        y_copy(m, u).wait_send()

    n_ops = sources_ref.shape[0]
    row = lax.broadcasted_iota(jnp.int32, sources_ref.shape, 0)
    entry = lax.broadcasted_iota(jnp.int32, sources_ref.shape, 1)
    live = jnp.zeros(sources_ref.shape, jnp.int32)
    for j in range(n_ops):
        live = jnp.where(row == j, count_ref[j], live)
    weighted = jnp.where(entry < live, integrals_ref[...], 0.0)
    for g in range(n_ops):
        hit = jnp.where(sources_ref[...] == slot_ref[g], weighted, 0.0)
        table[g] = jnp.broadcast_to(jnp.sum(hit, axis=1, keepdims=True), (n_ops, 128))

    def b_copy(m, u, slot):
        at, i = columns(u), u * n_pair + m
        return copy(b_out.at[m, :, :, at], out_ref.at[:, rows(slot * piece, piece), at],
                    b_s.at[i], b_r.at[i], dev(lax.rem(p + m, n_pair), s))

    for u in range(PARTS):
        for m in steps:
            if m:
                a_copy(m, u, lax.rem(p - m + n_pair, n_pair)).wait_recv()
        for m in steps:
            q = lax.rem(p + m, n_pair)
            for n in range(wide // PARTS // 128):
                at = pl.ds(u * (wide // PARTS) + n * 128, 128)
                for j in range(local):
                    total = None
                    for g in range(n_ops):
                        term = table[g, pl.ds(q * local + j, 1)] * a_in[g // local, g % local, :, at]
                        total = term if total is None else total + term
                    if m == 0:
                        out_ref[j, rows(p * piece, piece), at] = total
                    else:
                        b_out[m, j, :, at] = total
            if m:
                b_copy(m, u, p).start()
    for u, m in turns_away:
        a_copy(m, u, p).wait_send()
    for u, m in turns_away:
        b_copy(m, u, lax.rem(p - m + n_pair, n_pair)).wait_recv()
    for u, m in turns_away:
        b_copy(m, u, p).wait_send()


def fused(operators, rotation, owner, slot_pair, term_count, sources, integrals, n_pair):
    local, block, width = operators.shape
    wide = rotation.shape[1]
    half, new_rows = block // 2, wide // 4
    piece = new_rows // n_pair
    dma = pltpu.SemaphoreType.DMA
    vmem = pltpu.VMEM
    chain = [vmem((half, wide), F32)] * 6
    scratch = [vmem((local, block, width), F32), vmem((block, wide), F32),
               vmem((local * n_pair, local * n_pair, 128), F32), dma((2,))]
    scratch += [vmem((local * block, width), BF16)] * 2 + chain + [
        vmem((width, wide), F32),
        vmem((width, wide), BF16), vmem((width, wide), BF16),
        vmem((wide, block), BF16), vmem((wide, block), BF16),
        vmem((local * block, wide), BF16), vmem((local * block, wide), BF16),
        vmem((2, local, new_rows, wide), F32),
        vmem((2, local, new_rows, wide), F32),
        vmem((2, local, new_rows, wide), F32),
        vmem((n_pair, local, piece, wide), F32),
        vmem((n_pair, local, piece, wide), F32),
        vmem((n_pair, local, piece, wide), F32),
        vmem((n_pair, local, piece, wide), F32),
        vmem((n_pair, local, piece, wide), F32),
    ]
    links = CHUNKS + CHUNKS // 2
    counts = [CHUNKS] * 6 + [links] * 4 + [2 * CHUNKS] * 2 + [2 * local] * 2 + [PARTS * n_pair] * 6
    scratch += [dma((count,)) for count in counts]
    smem = pl.BlockSpec(memory_space=pltpu.SMEM)
    in_vmem = pl.BlockSpec(memory_space=pltpu.VMEM)
    return pl.pallas_call(
        functools.partial(kernel, n_pair),
        out_shape=pltpu.VMEM((local, new_rows, wide), F32),
        in_specs=[smem] * 3 + [in_vmem] * 2 + [pl.BlockSpec(memory_space=pl.ANY)] * 2,
        out_specs=in_vmem,
        scratch_shapes=scratch,
        compiler_params=pltpu.CompilerParams(
            collective_id=0, has_side_effects=True, vmem_limit_bytes=56 * 1024 * 1024
        ),
    )(owner, slot_pair, term_count, sources, integrals, operators, rotation)


def on_device(fits, operators, rotations, sector_owner, slot_pair, sources, integrals, term_count):
    sect_count = lax.axis_size("sect")
    pair_count = lax.axis_size("pair")
    local_ops = operators.shape[0]
    if fits:
        return fused(operators, rotations[0], sector_owner, slot_pair, term_count,
                     sources, integrals, pair_count)
    coupling = coupling_matrix(slot_pair, sources, integrals, term_count)
    own_block = broadcast(rotations[0], "pair", sector_owner[0])
    rotation_full = lax.all_gather(own_block, "sect", axis=0, tiled=True)
    width_new = rotation_full.shape[1]
    new_rows = width_new // sect_count
    highest = dict(precision=lax.Precision.HIGHEST, preferred_element_type=jnp.float32)
    right_done = jnp.einsum("oij,jb->oib", operators, rotation_full, **highest)
    columns = lax.dynamic_slice_in_dim(
        rotation_full, lax.axis_index("sect") * new_rows, new_rows, 1
    )
    rotated = jnp.einsum(
        "ia,oib->oab",
        columns,
        lax.all_gather(right_done, "sect", axis=1, tiled=True),
        **highest,
    )
    blocks = rotated.reshape(local_ops, pair_count, -1)
    mixture = jnp.einsum(
        "or,rhn->ohn",
        coupling,
        lax.all_to_all(blocks, "pair", split_axis=1, concat_axis=0, tiled=True),
        **highest,
    )
    result = lax.all_to_all(mixture, "pair", split_axis=0, concat_axis=1, tiled=True)
    return result.reshape(local_ops, new_rows, width_new)


def solution(mesh):
    pair_count, sect_count = mesh.shape["pair"], mesh.shape["sect"]

    def call(operators, rotations, *rest):
        wide = rotations.shape[2]
        fits = sect_count == 4 and pair_count % 2 == 0 and wide % (8 * pair_count * sect_count) == 0 and wide % (128 * PARTS) == 0
        in_specs = (P("pair", "sect", None), P("pair", "sect", None), P(), P(), P(), P(), P())
        return jax.shard_map(
            functools.partial(on_device, fits), mesh=mesh, in_specs=in_specs,
            out_specs=P("pair", "sect", None), check_vma=False,
        )(operators, rotations, *rest)

    return call
```

time: 105 us -> 104 us (level)
  no operation moved by 1% of the time
where the time goes in v3:
time: 104 us
  Pallas kernels  102 us (98%)
    pallas_call x1, Pallas kernels, fused(): pl.pallas_call(functools.partial(kernel, n_pair), out_shape=pltpu.VMEM((l...  102 us

profile of v3, /device:TPU:16, one launch (start us, length us, event | category | flops | bytes accessed | tf_op | source)
XLA Modules:
  0.0 104.1 jit_solution(15483144059131727797)
XLA Ops:
  0.7 102.5 %shard_map.73 = f32[2,192,768]{2,1,0:T(8,128)S(1)} custom-call(s32[1]{0:T(128)S(6)} %copy.10.owner_ref, s32[16]{0:T(128)} %slot_ref.1, s32[16]{0:T(128)} %count_ref.1, s32[16,16]{1,0:T(8,128)} %sources_ref.1, f32[16,16]{1,0:T(8,128)} %integrals_ref.1, f32[2,256,1024]{2,1,0:T(8,128)} %ops_in.1, f32[256,768]{1,0:T(8,128)} %bitcast.1), custom_call_target="tpu_custom_call" | custom-call | tf_op jit(solution)/shard_map/pallas_call | solution.py:377
  103.1 1.0 copy.9
